TPU v7x, 32 devices: a whole 2x2x4 slice. The times are simulated.
32 devices in a mesh: sa: 8 (over y, x, core), sb: 4 (over z).
Axes of the slice: x: 2, y: 2, z: 4, core: 2. Of those that a mesh axis runs over, the one named last changes fastest.
Arguments:
- spectra: bfloat16 [131072, 1024], P(('sa', 'sb')), as said below
- omega: int32 [1024, 256], replicated, may hold values from -4 to 4
Outputs:
- basis: bfloat16 [131072, 256], P(('sa', 'sb'))
- projected: float32 [256, 1024], replicated
Inputs may be any that keep to these rules, and one draw needn't show every extreme that they name: `spectra`: rows are full rank over the features.
All inputs are finite; a program needn't handle non-finite values.
Results may differ from a plain program's by a relative error of at most 0.002.
Values sent between devices are 32-bit elements; how exact they have to be, the bound alone decides.
A program may use at most 64 MiB of HBM per device.

v0:
```python
import jax
import jax.numpy as jnp
from jax import lax
from jax.sharding import PartitionSpec as P


def from_partner(block, axis, apart):
    count = lax.axis_size(axis)
    route = []
    for low in range(count):
        high = low | 1 << apart
        if high != low and high < count:
            route += [(low, high), (high, low)]
    return lax.ppermute(block, axis, route)


def sum_cross(partial_cross):
    return lax.psum(partial_cross, ("sa", "sb"))


def on_device(spectra, omega):
    rank = omega.shape[1]
    gain = (3.0 / (20.0 * spectra.shape[1])) ** 0.5
    total_rows = spectra.shape[0] * lax.axis_size("sa") * lax.axis_size("sb")
    root_rows = jnp.sqrt(jnp.float32(total_rows))
    sketch = jnp.dot(spectra, omega.astype(jnp.bfloat16), preferred_element_type=jnp.float32) * gain
    local_gram = jnp.dot(
        sketch.T, sketch, precision=lax.Precision.HIGHEST, preferred_element_type=jnp.float32
    )
    gram = local_gram
    for bit in range(lax.axis_size("sa").bit_length() - 1):
        gram = gram + from_partner(gram, "sa", bit)
    for bit in range(lax.axis_size("sb").bit_length() - 1):
        gram = gram + from_partner(gram, "sb", bit)
    lower = jnp.linalg.cholesky(gram)
    inverse = jax.scipy.linalg.solve_triangular(lower, jnp.eye(rank, dtype=jnp.float32), lower=True)
    basis = (
        jnp.dot(
            sketch, inverse.T, precision=lax.Precision.HIGHEST, preferred_element_type=jnp.float32
        )
        * root_rows
    ).astype(jnp.bfloat16)
    partial_proj = jnp.dot(basis.T, spectra, preferred_element_type=jnp.float32)
    summed = sum_cross(partial_proj)
    return (basis, summed / total_rows)


def solution(mesh):
    return jax.shard_map(
        on_device,
        mesh=mesh,
        in_specs=(P(("sa", "sb"), None), P()),
        out_specs=(P(("sa", "sb"), None), P()),
        check_vma=False,
    )
```

profile of v0, /device:TPU:1, one launch (start us, length us, event | category | flops | bytes accessed | tf_op | source)
XLA Modules:
  0.0 271.2 jit_solution(11106561071297860250)
XLA Ops:
  7.2 6.0 %convolution_multiply_fusion.1 = f32[4096,256]{1,0:T(8,128)S(1)} fusion(bf16[4096,1024]{1,0:T(8,128)(2,1)} %param.2, s32[1024,256]{1,0:T(8,128)} %param.3), kind=kOutput, calls=%fused_computation.3 | convolution fusion | flops 2148794368 | bytes 13631488 | tf_op jit(solution)/shard_map/dot_general | solution.py:26
  13.2 6.7 %fusion.15 = f32[256,256]{0,1:T(8,128)S(1)} fusion(f32[4096,256]{1,0:T(8,128)S(1)} %convolution_multiply_fusion.1), kind=kOutput, calls=%fused_computation.38 | convolution fusion | flops 3221225472 | bytes 4456448 | tf_op jit(solution)/shard_map/dot_general | solution.py:27
  19.9 0.1 collective-permute-start
  20.1 1.5 collective-permute-done
  21.6 2.4 collective-permute-start.1
  24.0 6.4 %collective-permute-done.1 = f32[256,256]{0,1:T(8,128)S(1)} collective-permute-done((f32[256,256]{0,1:T(8,128)S(1)}, f32[256,256]{0,1:T(8,128)S(1)}, u32[]{:S(2)}, u32[]{:S(2)}) %collective-permute-start.1) | collective-permute-done | bytes 262176 | tf_op jit(solution)/shard_map/ppermute | solution.py:14
  30.4 1.2 collective-permute-start.2
  31.6 5.8 %collective-permute-done.2 = f32[256,256]{0,1:T(8,128)S(1)} collective-permute-done((f32[256,256]{0,1:T(8,128)S(1)}, f32[256,256]{0,1:T(8,128)S(1)}, u32[]{:S(2)}, u32[]{:S(2)}) %collective-permute-start.2) | collective-permute-done | bytes 262176 | tf_op jit(solution)/shard_map/ppermute | solution.py:14
  37.4 1.0 collective-permute-start.3
  38.4 5.1 %collective-permute-done.3 = f32[256,256]{0,1:T(8,128)S(1)} collective-permute-done((f32[256,256]{0,1:T(8,128)S(1)}, f32[256,256]{0,1:T(8,128)S(1)}, u32[]{:S(2)}, u32[]{:S(2)}) %collective-permute-start.3) | collective-permute-done | bytes 262176 | tf_op jit(solution)/shard_map/ppermute | solution.py:14
  43.6 1.6 collective-permute-start.4
  45.2 12.8 %collective-permute-done.4 = f32[256,256]{0,1:T(8,128)S(1)} collective-permute-done((f32[256,256]{0,1:T(8,128)S(1)}, f32[256,256]{0,1:T(8,128)S(1)}, u32[]{:S(2)}, u32[]{:S(2)}) %collective-permute-start.4) | collective-permute-done | bytes 262176 | tf_op jit(solution)/shard_map/ppermute | solution.py:14
  58.1 0.1 copy.6
  58.3 11.8 %cholesky.50 = f32[128,128]{1,0:T(8,128)S(1)} custom-call(f32[128,128]{1,0:T(8,128)S(1)} %cholesky.118), custom_call_target="Cholesky" | custom-call | tf_op jit(solution)/shard_map/jit(cholesky)/cholesky | solution.py:35
  70.1 9.8 %custom-call.15 = f32[1,128,128]{1,2,0:T(8,128)S(1)} custom-call(f32[1,128,128]{2,1,0:T(8,128)S(1)} %get-tuple-element.23), custom_call_target="InvertDiagBlocksLowerTriangular" | custom-call | tf_op jit(solution)/shard_map/jit(cholesky)/cholesky | solution.py:35
  80.0 0.2 constant_dynamic-update-slice_fusion.1
  80.2 0.3 slice_subtract_fusion
  80.5 11.7 %cholesky.105 = f32[128,128]{1,0:T(8,128)S(1)} custom-call(f32[128,128]{1,0:T(8,128)S(1)} %slice_subtract_fusion), custom_call_target="Cholesky" | custom-call | tf_op jit(solution)/shard_map/jit(cholesky)/cholesky | solution.py:35
  92.2 0.7 compare_reduce_fusion
  94.4 4.3 %while.1 = (s32[]{:T(128)}, f32[256,256]{1,0:T(8,128)S(1)}, s32[2,2]{1,0:T(2,128)S(1)}, f32[2,128,128]{2,1,0:T(8,128)S(1)}, s32[]{:T(128)}) while((s32[]{:T(128)}, f32[256,256]{1,0:T(8,128)S(1)}, s32[2,2]{1,0:T(2,128)S(1)}, f32[2,128,128]{2,1,0:T(8,128)S(1)}, s32[]{:T(128)}) %tuple.27), condition=%wide.while_cond, body=%wide.while_body.sunk | while | flops 2 | bytes 131189 | solution.py:36
  94.6 0.6 fusion.28
  95.2 1.4 bitcast_dynamic-update-slice_fusion.2
  96.6 0.6 fusion.28
  97.2 1.4 bitcast_dynamic-update-slice_fusion.2
  98.7 19.7 %custom-call.16 = f32[2,128,128]{1,2,0:T(8,128)S(1)} custom-call(f32[2,128,128]{2,1,0:T(8,128)S(1)} %get-tuple-element.9), custom_call_target="InvertDiagBlocksLowerTriangular" | custom-call | tf_op jit(solution)/shard_map/jit(_solve_triangular)/triangular_solve | solution.py:36
  118.4 0.3 fusion.6
  118.6 0.3 convolution_subtract_fusion
  118.9 0.3 fusion.9
  119.2 5.7 %fusion = bf16[4096,256]{1,0:T(8,128)(2,1)S(1)} fusion(f32[4096,256]{1,0:T(8,128)} %copy-done, f32[128,256]{1,0:T(8,128)S(1)} %fusion.9, f32[128,256]{1,0:T(8,128)S(1)} %fusion.6), kind=kOutput, calls=%fused_computation.4 | convolution fusion | flops 3223388160 | bytes 6553600 | tf_op jit(solution)/shard_map/dot_general | solution.py:38
  124.9 7.5 %fusion.16 = f32[256,1024]{1,0:T(8,128)} fusion(bf16[4096,256]{1,0:T(8,128)(2,1)S(1)} %fusion, bf16[4096,1024]{1,0:T(8,128)(2,1)} %param.2), kind=kOutput, calls=%fused_computation.39 | convolution fusion | flops 2147483648 | bytes 11534336 | tf_op jit(solution)/shard_map/dot_general | solution.py:43
  132.4 129.6 %all-reduce.3.cloned.1.call-done = f32[256,1024]{1,0:T(8,128)} async-done(((f32[256,1024]{1,0:T(8,128)}), f32[256,1024]{1,0:T(8,128)}) %all-reduce.3.cloned.1.call-update) | async-done | bytes 1048592 | tf_op jit(solution)/shard_map/psum | solution.py:18
  262.0 2.3 broadcast_multiply_fusion
  (23 shorter events, 0.5 us)
Async XLA Ops:
  7.2 254.9 %all-reduce.3.cloned.1.call-start = ((), (), s32[]{:S(2)}) async-start(), calls=%async_computation | async-start | bytes 2097152 | tf_op jit(solution)/shard_map/psum | solution.py:18
  13.2 6.7 %copy-start = (f32[4096,256]{1,0:T(8,128)}, f32[4096,256]{1,0:T(8,128)S(1)}, u32[]{:S(2)}) copy-start(f32[4096,256]{1,0:T(8,128)S(1)} %convolution_multiply_fusion.1) | copy-start | bytes 12582916
  19.9 1.6 collective-permute-start
  21.6 8.8 %collective-permute-start.1 = (f32[256,256]{0,1:T(8,128)S(1)}, f32[256,256]{0,1:T(8,128)S(1)}, u32[]{:S(2)}, u32[]{:S(2)}) collective-permute-start(f32[256,256]{0,1:T(8,128)S(1)} %add.40), channel_id=1, source_target_pairs={{0,8},{8,0},{4,12},{12,4},{16,24},{24,16},{20,28},{28,20},{1,9},{9... | collective-permute-start | bytes 786440 | tf_op jit(solution)/shard_map/ppermute | solution.py:14
  30.4 7.0 %collective-permute-start.2 = (f32[256,256]{0,1:T(8,128)S(1)}, f32[256,256]{0,1:T(8,128)S(1)}, u32[]{:S(2)}, u32[]{:S(2)}) collective-permute-start(f32[256,256]{0,1:T(8,128)S(1)} %add.41), channel_id=1, source_target_pairs={{0,16},{16,0},{4,20},{20,4},{8,24},{24,8},{12,28},{28,12},{1,17},{... | collective-permute-start | bytes 786440 | tf_op jit(solution)/shard_map/ppermute | solution.py:14
  37.4 6.1 %collective-permute-start.3 = (f32[256,256]{0,1:T(8,128)S(1)}, f32[256,256]{0,1:T(8,128)S(1)}, u32[]{:S(2)}, u32[]{:S(2)}) collective-permute-start(f32[256,256]{0,1:T(8,128)S(1)} %add.42), channel_id=1, source_target_pairs={{0,1},{1,0},{2,3},{3,2},{4,5},{5,4},{6,7},{7,6},{8,9},{9,8},{10,11... | collective-permute-start | bytes 786440 | tf_op jit(solution)/shard_map/ppermute | solution.py:14
  43.6 14.5 %collective-permute-start.4 = (f32[256,256]{0,1:T(8,128)S(1)}, f32[256,256]{0,1:T(8,128)S(1)}, u32[]{:S(2)}, u32[]{:S(2)}) collective-permute-start(f32[256,256]{0,1:T(8,128)S(1)} %add.43), channel_id=1, source_target_pairs={{0,2},{2,0},{1,3},{3,1},{4,6},{6,4},{5,7},{7,5},{8,10},{10,8},{9,1... | collective-permute-start | bytes 786440 | tf_op jit(solution)/shard_map/ppermute | solution.py:14
  124.9 7.5 %copy-start.1 = (bf16[4096,256]{1,0:T(8,128)(2,1)}, bf16[4096,256]{1,0:T(8,128)(2,1)S(1)}, u32[]{:S(2)}) copy-start(bf16[4096,256]{1,0:T(8,128)(2,1)S(1)} %fusion) | copy-start | bytes 6291460
Sparse Core Ops, SparseCore 0:
  132.5 129.4 all-reduce.2
where the time goes:
time: 273 us; the launch traced here: 271 us
  waiting for transfers between devices  161 us (59%)
  other arithmetic  56.4 us (21%)
  matrix products  27.1 us (10%)
  between operations  15.5 us (6%)
  starting transfers between devices  6.37 us (2%)
  local copies, waits for them, and re-layouts  4.29 us (2%)
    psum x1, waiting for transfers between devices, sum_cross(): return lax.psum(partial_cross, ('sa', 'sb'))  130 us
    another operation x6, other arithmetic, on_device(): lower = jnp.linalg.cholesky(gram)  34.2 us
    ppermute x5, waiting for transfers between devices, from_partner(): return lax.ppermute(block, axis, route)  31.6 us
    another operation x3, other arithmetic, on_device(): jax.scipy.linalg.solve_triangular(lower, jnp.eye(rank, dtype=jnp.float32)...  19.7 us
    dot_general x1, matrix products, on_device(): partial_proj = jnp.dot(basis.T, spectra, preferred_element_type=jnp.float32)  7.47 us
    dot_general x1, matrix products, on_device(): jnp.dot(sketch.T, sketch, precision=lax.Precision.HIGHEST, preferred_elem...  6.72 us
    ppermute x5, starting transfers between devices, from_partner(): return lax.ppermute(block, axis, route)  6.33 us
    dot_general x1, matrix products, on_device(): jnp.dot(spectra, omega.astype(jnp.bfloat16), preferred_element_type=jnp.f...  5.97 us
  transfers between devices with their start and end apart: 6, of which 6 were waited for; matrix products, arithmetic and copies ran while one was open for 0% of the time, Pallas kernels for 0%

commit v1 on v0

v1 whole, which is shorter than its diff:
```python
import functools

import jax
import jax.numpy as jnp
from jax import lax
from jax.experimental import pallas as pl
from jax.experimental.pallas import tpu as pltpu
from jax.sharding import PartitionSpec as P

F32 = jnp.float32
BF16 = jnp.bfloat16
PANEL = 32
LEAF = 8
CHUNK = 512
COLS = 256


def dot(a, b, ca=1, cb=0):
    return lax.dot_general(a, b, (((ca,), (cb,)), ((), ())), preferred_element_type=F32)


def split2(a):
    high = a.astype(BF16)
    return high, (a - high.astype(F32)).astype(BF16)


def split3(a):
    high, rest = a.astype(BF16), None
    rest = a - high.astype(F32)
    mid = rest.astype(BF16)
    return high, mid, (rest - mid.astype(F32)).astype(BF16)


def dot_f32(a, b):
    a1, a2, a3 = split3(a)
    b1, b2, b3 = split3(b)
    return dot(
        jnp.concatenate([a1, a1, a1, a2, a2, a3], axis=1),
        jnp.concatenate([b1, b2, b3, b1, b2, b1], axis=0),
    )


def rank_update(u, v):
    a1, a2, a3 = split3(u)
    b1, b2, b3 = split3(v)
    return dot(
        jnp.concatenate([a1, a1, a1, a2, a2, a3], axis=0),
        jnp.concatenate([b1, b2, b3, b1, b2, b1], axis=0),
        0,
        0,
    )


def leaf_inverse(block, first):
    a = {}
    for j in range(LEAF):
        column = jnp.broadcast_to(block[:, first + j : first + j + 1], (LEAF, 128))
        for i in range(j, LEAF):
            a[i, j] = jnp.broadcast_to(column[i : i + 1, :], (LEAF, 128))
    low, inv = {}, {}
    for j in range(LEAF):
        inv[j, j] = lax.rsqrt(a[j, j])
        for i in range(j + 1, LEAF):
            low[i, j] = a[i, j] * inv[j, j]
        for k in range(j + 1, LEAF):
            for i in range(k, LEAF):
                a[i, k] = a[i, k] - low[i, j] * low[k, j]
    for j in range(LEAF):
        for i in range(j + 1, LEAF):
            total = low[i, j] * inv[j, j]
            for k in range(j + 1, i):
                total = total + low[i, k] * inv[k, j]
            inv[i, j] = -total * inv[i, i]
    return inv


def factor_panel(block):
    sub = lax.broadcasted_iota(jnp.int32, (LEAF, 128), 0)
    tiles = [block[LEAF * q : LEAF * (q + 1), :] for q in range(PANEL // LEAF)]
    count = len(tiles)
    for q in range(count):
        inv = leaf_inverse(tiles[q], LEAF * q)
        scaled = jnp.zeros((LEAF, 128), F32)
        for j in range(LEAF):
            column = inv[LEAF - 1, j]
            for i in range(LEAF - 2, j - 1, -1):
                column = jnp.where(sub == i, inv[i, j], column)
            if j:
                column = jnp.where(sub < j, 0.0, column)
            scaled = scaled + column * jnp.broadcast_to(tiles[q][j : j + 1, :], (LEAF, 128))
        raw = {}
        for s in range(q + 1, count):
            for j in range(LEAF):
                lane = LEAF * q + j
                raw[s, j] = jnp.broadcast_to(tiles[s][:, lane : lane + 1], (LEAF, 128))
        for s in range(q + 1, count):
            value = tiles[s]
            for j in range(LEAF):
                factor = raw[s, 0] * inv[j, 0]
                for k in range(1, j + 1):
                    factor = factor + raw[s, k] * inv[j, k]
                value = value - factor * jnp.broadcast_to(scaled[j : j + 1, :], (LEAF, 128))
            tiles[s] = value
        tiles[q] = scaled
    return jnp.concatenate(tiles, axis=0)


def factor_step(k, work, inverse):
    rank = work.shape[0]
    rows = pl.ds(pl.multiple_of(k * PANEL, PANEL), PANEL)
    panel = work[rows, :]
    turned = pltpu.roll(panel[:, :rank], lax.rem(rank - k * PANEL, rank), 1)[:, :128]
    lane = lax.broadcasted_iota(jnp.int32, (PANEL, 128), 1)
    sub = lax.broadcasted_iota(jnp.int32, (PANEL, 128), 0)
    block = jnp.where(lane < PANEL, turned, jnp.where(lane == sub + PANEL, 1.0, 0.0))
    small = factor_panel(block)[:, PANEL : 2 * PANEL]
    done = dot_f32(small, panel)
    inverse[rows, :] = done[:, rank:]
    work[...] = work[...] - rank_update(done[:, :rank], done)


def factor_init(gram, work):
    rank = gram.shape[0]
    sub = lax.broadcasted_iota(jnp.int32, (rank, rank), 0)
    lane = lax.broadcasted_iota(jnp.int32, (rank, rank), 1)
    work[:, :rank] = gram
    work[:, rank:] = jnp.where(sub == lane, 1.0, 0.0)


def kernel(
    n_sa, n_sb,
    x_hbm, omega_ref, basis_ref, proj_ref,
    x_v, hi_v, lo_v, hit_v, lot_v, om_v, hh_v, hl_v, gram_v, cross_v,
    gbuf, zbuf, gfull, cbuf, cpart, czbuf, cfull, work, inverse,
    x_sem, send_sem, recv_sem,
):
    rows, features = x_hbm.shape
    rank = omega_ref.shape[1]
    share = rank // n_sa
    per_tile = n_sb // (share // 8)
    width = features // per_tile
    total_rows = rows * n_sa * n_sb
    gain = (3.0 / (20.0 * features)) ** 0.5
    chunks = rows // CHUNK
    a_me, b_me = lax.axis_index("sa"), lax.axis_index("sb")

    def x_copy(i):
        part = pl.ds(pl.multiple_of(i * CHUNK, CHUNK), CHUNK)
        return pltpu.make_async_copy(x_hbm.at[part], x_v.at[part], x_sem.at[i])

    for i in range(chunks):
        x_copy(i).start()

    def start(phase, axis, count, me, source, target):
        copies = []
        for p in range(1, count):
            peer = lax.rem(me + p, count)
            copy = pltpu.make_async_remote_copy(
                src_ref=source(peer),
                dst_ref=target,
                send_sem=send_sem.at[phase, p],
                recv_sem=recv_sem.at[phase, p],
                device_id={axis: peer},
                device_id_type=pl.DeviceIdType.MESH,
            )
            copy.start()
            copies.append(copy)
        return copies

    def finish(copies):
        for copy in copies:
            copy.wait()

    barrier = pltpu.get_barrier_semaphore()
    for p in range(1, n_sa):
        pl.semaphore_signal(
            barrier, inc=1, device_id={"sa": lax.rem(a_me + p, n_sa)}, device_id_type=pl.DeviceIdType.MESH
        )
    for p in range(1, n_sb):
        pl.semaphore_signal(
            barrier, inc=1, device_id={"sb": lax.rem(b_me + p, n_sb)}, device_id_type=pl.DeviceIdType.MESH
        )

    om_v[...] = omega_ref[...].astype(F32).astype(BF16)
    hh_v[...] = jnp.zeros_like(hh_v)
    hl_v[...] = jnp.zeros_like(hl_v)

    @pl.loop(0, chunks)
    def _(i):
        x_copy(i).wait()
        part = pl.ds(pl.multiple_of(i * CHUNK, CHUNK), CHUNK)
        sketch = dot(x_v[part, :], om_v[...]) * gain
        hi, lo = split2(sketch)
        hi_t, lo_t = split2(sketch.T)
        hi_v[part, :] = hi
        lo_v[part, :] = lo
        hit_v[:, part] = hi_t
        lot_v[:, part] = lo_t
        hh_v[...] += dot(hi_t, hi)
        hl_v[...] += dot(hi_t, lo)

    cut = lambda i: pl.ds(pl.multiple_of(i * share, share), share)
    gram_v[...] = hh_v[...] + (hl_v[...] + hl_v[...].T)

    pl.semaphore_wait(barrier, n_sa - 1 + n_sb - 1)
    copies = start(0, "sa", n_sa, a_me, lambda t: gram_v.at[cut(t)], gbuf.at[a_me])
    gbuf[a_me] = gram_v[cut(a_me), :]

    def cross(begin, end):
        @pl.loop(begin, end)
        def _(i):
            block = pl.ds(pl.multiple_of(i * COLS, COLS), COLS)
            x = x_v[:, block]
            cross_v[:, block] = dot(hit_v[...], x) + dot(lot_v[...], x)

    blocks = features // COLS
    cross(0, blocks // 2)

    def total(buffer, count):
        value = buffer[0]
        for i in range(1, count):
            value = value + buffer[i]
        return value

    finish(copies)
    zbuf[b_me] = total(gbuf, n_sa)
    copies = start(1, "sb", n_sb, b_me, lambda t: zbuf.at[b_me], zbuf.at[b_me])
    cross(blocks // 2, blocks)
    finish(copies)
    gfull[cut(a_me), :] = total(zbuf, n_sb)
    copies = start(2, "sa", n_sa, a_me, lambda t: gfull.at[cut(a_me)], gfull.at[cut(a_me)])
    c_copies = start(3, "sa", n_sa, a_me, lambda t: cross_v.at[cut(t)], cbuf.at[a_me])
    cbuf[a_me] = cross_v[cut(a_me), :]
    finish(copies)

    factor_init(gfull[...], work)
    panels = rank // PANEL

    def factor(begin, end):
        @pl.loop(begin, end)
        def _(k):
            factor_step(k, work, inverse)

    def piece(t, first):
        return (
            pl.ds(pl.multiple_of(first + lax.div(t, per_tile) * 8, 8), 8),
            pl.ds(pl.multiple_of(lax.rem(t, per_tile) * width, width), width),
        )

    factor(0, panels * 3 // 8)
    finish(c_copies)
    cpart[...] = total(cbuf, n_sa)
    copies = start(4, "sb", n_sb, b_me, lambda t: cpart.at[piece(t, 0)], czbuf.at[b_me])
    czbuf[b_me] = cpart[piece(b_me, 0)]
    factor(panels * 3 // 8, panels * 5 // 8)
    finish(copies)
    mine = piece(b_me, a_me * share)
    cfull[mine] = total(czbuf, n_sb)
    copies = start(5, "sb", n_sb, b_me, lambda t: cfull.at[mine], cfull.at[mine])
    factor(panels * 5 // 8, panels * 7 // 8)
    finish(copies)
    copies = start(6, "sa", n_sa, a_me, lambda t: cfull.at[cut(a_me)], cfull.at[cut(a_me)])
    factor(panels * 7 // 8, panels)

    inv_hi, inv_lo = split2(inverse[...])
    root = float(total_rows) ** 0.5

    @pl.loop(0, chunks)
    def _(i):
        part = pl.ds(pl.multiple_of(i * CHUNK, CHUNK), CHUNK)
        hi = hi_v[part, :]
        value = dot(hi, inv_hi, 1, 1) + (dot(hi, inv_lo, 1, 1) + dot(lo_v[part, :], inv_hi, 1, 1))
        basis_ref[part, :] = (value * root).astype(BF16)

    finish(copies)
    scale = root / total_rows

    @pl.loop(0, blocks)
    def _(i):
        block = pl.ds(pl.multiple_of(i * COLS, COLS), COLS)
        hi, lo = split2(cfull[:, block])
        proj_ref[:, block] = (dot(inv_hi, hi) + (dot(inv_hi, lo) + dot(inv_lo, hi))) * scale


def on_device(spectra, omega):
    rows, features = spectra.shape
    rank = omega.shape[1]
    n_sa, n_sb = lax.axis_size("sa"), lax.axis_size("sb")
    share = rank // n_sa
    width = features * (share // 8) // n_sb
    vmem = pltpu.VMEM
    return pl.pallas_call(
        functools.partial(kernel, n_sa, n_sb),
        out_shape=(
            jax.ShapeDtypeStruct((rows, rank), BF16),
            jax.ShapeDtypeStruct((rank, features), F32),
        ),
        in_specs=[pl.BlockSpec(memory_space=pl.ANY), pl.BlockSpec(memory_space=pltpu.VMEM)],
        out_specs=(pl.BlockSpec(memory_space=pltpu.VMEM), pl.BlockSpec(memory_space=pltpu.VMEM)),
        scratch_shapes=[
            vmem((rows, features), BF16),
            vmem((rows, rank), BF16),
            vmem((rows, rank), BF16),
            vmem((rank, rows), BF16),
            vmem((rank, rows), BF16),
            vmem((features, rank), BF16),
            vmem((rank, rank), F32),
            vmem((rank, rank), F32),
            vmem((rank, rank), F32),
            vmem((rank, features), F32),
            vmem((n_sa, share, rank), F32),
            vmem((n_sb, share, rank), F32),
            vmem((rank, rank), F32),
            vmem((n_sa, share, features), F32),
            vmem((share, features), F32),
            vmem((n_sb, 8, width), F32),
            vmem((rank, features), F32),
            vmem((rank, 2 * rank), F32),
            vmem((rank, rank), F32),
            pltpu.SemaphoreType.DMA((rows // CHUNK,)),
            pltpu.SemaphoreType.DMA((7, max(n_sa, n_sb))),
            pltpu.SemaphoreType.DMA((7, max(n_sa, n_sb))),
        ],
        compiler_params=pltpu.CompilerParams(
            collective_id=0, has_side_effects=True, vmem_limit_bytes=52 * 2**20
        ),
    )(spectra, omega)


def solution(mesh):
    return jax.shard_map(
        on_device,
        mesh=mesh,
        in_specs=(P(("sa", "sb"), None), P()),
        out_specs=(P(("sa", "sb"), None), P()),
        check_vma=False,
    )
```

time: 273 us -> 66.5 us (0.24)
  waiting for transfers between devices: 161 us -> 0 us
  Pallas kernels: 0 us -> 61.6 us
  other arithmetic: 56.4 us -> 0 us
  matrix products: 27.1 us -> 0 us
  between operations: 15.5 us -> 0.64 us
  starting transfers between devices: 6.37 us -> 0 us
    psum x1 -> x0, waiting for transfers between devices: 130 us -> none  [sum_cross(): return lax.psum(partial_cross, ('sa', 'sb'))]
    pallas_call x0 -> x1, Pallas kernels: none -> 61.6 us  [on_device(): pl.pallas_call(functools.partial(kernel, n_sa, n_sb), out_shape=(jax.Shap...]
    another operation x9 -> x0, other arithmetic: 53.9 us -> none  [the longest x6 34.2 us: on_device(): lower = jnp.linalg.cholesky(gram)]
    ppermute x5 -> x0, waiting for transfers between devices: 31.6 us -> none  [from_partner(): return lax.ppermute(block, axis, route)]
    dot_general x4 -> x0, matrix products: 25.8 us -> none  [the longest x1 7.47 us: on_device(): partial_proj = jnp.dot(basis.T, spectra, preferred_element_type=jnp.float32)]
    ppermute x5 -> x0, starting transfers between devices: 6.33 us -> none  [from_partner(): return lax.ppermute(block, axis, route)]
    another operation x9 -> x0, local copies, waits for them, and re-layouts: 4.15 us -> none
    unnamed x4 -> x2, local copies, waits for them, and re-layouts: 0.01 us -> 4.01 us
  transfers between devices with their start and end apart: 6 -> 0, of which waited for: 6 -> 0; matrix products, arithmetic and copies ran while one was open for 0% -> 0% of each run, Pallas kernels for 0% -> 0%
where the time goes in v1:
time: 66.5 us; the launch traced here: 66.3 us
  Pallas kernels  61.6 us (93%)
  local copies, waits for them, and re-layouts  4.01 us (6%)
    pallas_call x1, Pallas kernels, on_device(): pl.pallas_call(functools.partial(kernel, n_sa, n_sb), out_shape=(jax.Shap...  61.6 us
    unnamed x2, local copies, waits for them, and re-layouts  4.01 us

profile of v1, /device:TPU:1, one launch (start us, length us, event | category | flops | bytes accessed | tf_op | source)
XLA Modules:
  0.0 66.3 jit_solution(10926484632506113704)
XLA Ops:
  0.6 61.6 %shard_map.41 = (bf16[4096,256]{1,0:T(8,128)(2,1)}, f32[256,1024]{1,0:T(8,128)S(1)}) custom-call(bf16[4096,1024]{1,0:T(8,128)(2,1)} %x_hbm.1, s32[1024,256]{1,0:T(8,128)} %omega_ref.1), custom_call_target="tpu_custom_call" | custom-call | tf_op jit(solution)/shard_map/pallas_call | solution.py:292
  62.3 3.0 %copy.6 = bf16[4096,256]{1,0:T(8,128)(2,1)} copy(bf16[4096,256]{1,0:T(8,128)(2,1)} %get-tuple-element.4) | data formatting | bytes 4194304
  65.3 1.0 %copy.7 = f32[256,1024]{1,0:T(8,128)} copy(f32[256,1024]{1,0:T(8,128)S(1)} %get-tuple-element.5) | data formatting | bytes 2097152

commit v2 on v1

--- a/solution.py
+++ b/solution.py
@@ -128,30 +128,35 @@
 
 
 def kernel(
-    n_sa, n_sb,
-    x_hbm, omega_ref, basis_ref, proj_ref,
+    n_sa, n_sb, pieces,
+    x_hbm, omega_ref, hi_out, lo_out, cross_out, inverse,
     x_v, hi_v, lo_v, hit_v, lot_v, om_v, hh_v, hl_v, gram_v, cross_v,
-    gbuf, zbuf, gfull, cbuf, cpart, czbuf, cfull, work, inverse,
-    x_sem, send_sem, recv_sem,
+    gbuf, zbuf, gfull, pairbuf, cbuf, cpart, czbuf, cfull, work,
+    x_sem, out_sem, send_sem, recv_sem,
 ):
     rows, features = x_hbm.shape
     rank = omega_ref.shape[1]
     share = rank // n_sa
+    half = rank // 2
+    chips = n_sa // 2
+    wide = features // pieces
     per_tile = n_sb // (share // 8)
-    width = features // per_tile
-    total_rows = rows * n_sa * n_sb
+    width = wide // per_tile
     gain = (3.0 / (20.0 * features)) ** 0.5
     chunks = rows // CHUNK
     a_me, b_me = lax.axis_index("sa"), lax.axis_index("sb")
+    chip, core = lax.div(a_me, 2), lax.rem(a_me, 2)
+
+    def chunk(i):
+        return pl.ds(pl.multiple_of(i * CHUNK, CHUNK), CHUNK)
 
     def x_copy(i):
-        part = pl.ds(pl.multiple_of(i * CHUNK, CHUNK), CHUNK)
-        return pltpu.make_async_copy(x_hbm.at[part], x_v.at[part], x_sem.at[i])
+        return pltpu.make_async_copy(x_hbm.at[chunk(i)], x_v.at[chunk(i)], x_sem.at[i])
 
     for i in range(chunks):
         x_copy(i).start()
 
-    def start(phase, axis, count, me, source, target):
+    def start(phase, axis, count, me, source, target, device=lambda t: t):
         copies = []
         for p in range(1, count):
             peer = lax.rem(me + p, count)
@@ -160,7 +165,7 @@
                 dst_ref=target,
                 send_sem=send_sem.at[phase, p],
                 recv_sem=recv_sem.at[phase, p],
-                device_id={axis: peer},
+                device_id={axis: device(peer)},
                 device_id_type=pl.DeviceIdType.MESH,
             )
             copy.start()
@@ -188,7 +193,7 @@
     @pl.loop(0, chunks)
     def _(i):
         x_copy(i).wait()
-        part = pl.ds(pl.multiple_of(i * CHUNK, CHUNK), CHUNK)
+        part = chunk(i)
         sketch = dot(x_v[part, :], om_v[...]) * gain
         hi, lo = split2(sketch)
         hi_t, lo_t = split2(sketch.T)
@@ -199,22 +204,15 @@
         hh_v[...] += dot(hi_t, hi)
         hl_v[...] += dot(hi_t, lo)
 
-    cut = lambda i: pl.ds(pl.multiple_of(i * share, share), share)
-    gram_v[...] = hh_v[...] + (hl_v[...] + hl_v[...].T)
-
-    pl.semaphore_wait(barrier, n_sa - 1 + n_sb - 1)
-    copies = start(0, "sa", n_sa, a_me, lambda t: gram_v.at[cut(t)], gbuf.at[a_me])
-    gbuf[a_me] = gram_v[cut(a_me), :]
-
-    def cross(begin, end):
-        @pl.loop(begin, end)
-        def _(i):
-            block = pl.ds(pl.multiple_of(i * COLS, COLS), COLS)
-            x = x_v[:, block]
-            cross_v[:, block] = dot(hit_v[...], x) + dot(lot_v[...], x)
-
-    blocks = features // COLS
-    cross(0, blocks // 2)
+    outs = [
+        pltpu.make_async_copy(hi_v, hi_out, out_sem.at[0]),
+        pltpu.make_async_copy(lo_v, lo_out, out_sem.at[1]),
+    ]
+    for copy in outs:
+        copy.start()
+
+    def cut(i):
+        return pl.ds(pl.multiple_of(i * share, share), share)
 
     def total(buffer, count):
         value = buffer[0]
@@ -222,18 +220,81 @@
             value = value + buffer[i]
         return value
 
-    finish(copies)
-    zbuf[b_me] = total(gbuf, n_sa)
-    copies = start(1, "sb", n_sb, b_me, lambda t: zbuf.at[b_me], zbuf.at[b_me])
-    cross(blocks // 2, blocks)
-    finish(copies)
-    gfull[cut(a_me), :] = total(zbuf, n_sb)
-    copies = start(2, "sa", n_sa, a_me, lambda t: gfull.at[cut(a_me)], gfull.at[cut(a_me)])
-    c_copies = start(3, "sa", n_sa, a_me, lambda t: cross_v.at[cut(t)], cbuf.at[a_me])
-    cbuf[a_me] = cross_v[cut(a_me), :]
-    finish(copies)
-
-    factor_init(gfull[...], work)
+    gram_v[...] = hh_v[...] + (hl_v[...] + hl_v[...].T)
+    pl.semaphore_wait(barrier, n_sa - 1 + n_sb - 1)
+    gram_copies = start(0, "sa", n_sa, a_me, lambda t: gram_v.at[cut(t)], gbuf.at[a_me])
+    gbuf[a_me] = gram_v[cut(a_me), :]
+
+    def half_of(c):
+        return pl.ds(pl.multiple_of(c * half, half), half)
+
+    def owned(t):
+        first = core * half + t * share
+        return pl.ds(pl.multiple_of(first, share), share)
+
+    mine = owned(chip)
+
+    def spot(t, first):
+        return (
+            pl.ds(pl.multiple_of(first + lax.div(t, per_tile) * 8, 8), 8),
+            pl.ds(pl.multiple_of(lax.rem(t, per_tile) * width, width), width),
+        )
+
+    def same_core(t):
+        return 2 * t + core
+
+    def stages(h):
+        base = 3 + 6 * h
+        product, full = cross_v.at[h], cfull.at[h]
+
+        def compute():
+            for block in range(h * wide, (h + 1) * wide, COLS):
+                x = x_v[:, block : block + COLS]
+                part = slice(block - h * wide, block - h * wide + COLS)
+                cross_v[h, :, part] = dot(hit_v[...], x) + dot(lot_v[...], x)
+            return start(
+                base, "sa", 2, core, lambda t: product.at[half_of(t)], pairbuf.at[h], lambda t: 2 * chip + t
+            )
+
+        def plane_sum():
+            cross_v[h, half_of(core), :] += pairbuf[h]
+            copies = start(
+                base + 1, "sa", chips, chip, lambda t: product.at[owned(t)], cbuf.at[h, chip], same_core
+            )
+            cbuf[h, chip] = cross_v[h, mine, :]
+            return copies
+
+        def z_sum():
+            cpart[h] = total(cbuf.at[h], chips)
+            copies = start(
+                base + 2, "sb", n_sb, b_me, lambda t: cpart.at[h].at[spot(t, 0)], czbuf.at[h, b_me]
+            )
+            czbuf[h, b_me] = cpart.at[h][spot(b_me, 0)]
+            return copies
+
+        def z_gather():
+            place = spot(b_me, core * half + chip * share)
+            full[place] = total(czbuf.at[h], n_sb)
+            return start(base + 3, "sb", n_sb, b_me, lambda t: full.at[place], full.at[place])
+
+        def plane_gather():
+            return start(base + 4, "sa", chips, chip, lambda t: full.at[mine], full.at[mine], same_core)
+
+        def pair_gather():
+            held = full.at[half_of(core)]
+            return start(base + 5, "sa", 2, core, lambda t: held, held, lambda t: 2 * chip + t)
+
+        return [compute, plane_sum, z_sum, z_gather, plane_gather, pair_gather]
+
+    plan = [stages(h) for h in range(pieces)]
+    flight = [[] for _ in range(pieces)]
+
+    def advance(stage, *which):
+        for h in which or range(pieces):
+            if h < pieces:
+                finish(flight[h])
+                flight[h] = plan[h][stage]()
+
     panels = rank // PANEL
 
     def factor(begin, end):
@@ -241,45 +302,51 @@
         def _(k):
             factor_step(k, work, inverse)
 
-    def piece(t, first):
-        return (
-            pl.ds(pl.multiple_of(first + lax.div(t, per_tile) * 8, 8), 8),
-            pl.ds(pl.multiple_of(lax.rem(t, per_tile) * width, width), width),
+    advance(0, 0)
+    finish(gram_copies)
+    zbuf[b_me] = total(gbuf, n_sa)
+    gram_copies = start(1, "sb", n_sb, b_me, lambda t: zbuf.at[b_me], zbuf.at[b_me])
+    advance(1, 0)
+    advance(0, 1)
+    finish(gram_copies)
+    gfull[cut(a_me), :] = total(zbuf, n_sb)
+    gram_copies = start(2, "sa", n_sa, a_me, lambda t: gfull.at[cut(a_me)], gfull.at[cut(a_me)])
+    advance(1, 1)
+    advance(2, 0)
+    finish(gram_copies)
+    factor_init(gfull[...], work)
+    factor(0, 1)
+    advance(2, 1)
+    advance(3, 0)
+    factor(1, 3)
+    advance(3, 1)
+    advance(4, 0)
+    factor(3, 5)
+    advance(4, 1)
+    factor(5, 6)
+    advance(5, 0)
+    factor(6, panels)
+    advance(5, 1)
+    for h in range(pieces):
+        finish(flight[h])
+        outs.append(
+            pltpu.make_async_copy(
+                cfull.at[h], cross_out.at[:, pl.ds(h * wide, wide)], out_sem.at[2 + h]
+            )
         )
-
-    factor(0, panels * 3 // 8)
-    finish(c_copies)
-    cpart[...] = total(cbuf, n_sa)
-    copies = start(4, "sb", n_sb, b_me, lambda t: cpart.at[piece(t, 0)], czbuf.at[b_me])
-    czbuf[b_me] = cpart[piece(b_me, 0)]
-    factor(panels * 3 // 8, panels * 5 // 8)
-    finish(copies)
-    mine = piece(b_me, a_me * share)
-    cfull[mine] = total(czbuf, n_sb)
-    copies = start(5, "sb", n_sb, b_me, lambda t: cfull.at[mine], cfull.at[mine])
-    factor(panels * 5 // 8, panels * 7 // 8)
-    finish(copies)
-    copies = start(6, "sa", n_sa, a_me, lambda t: cfull.at[cut(a_me)], cfull.at[cut(a_me)])
-    factor(panels * 7 // 8, panels)
-
-    inv_hi, inv_lo = split2(inverse[...])
+        outs[-1].start()
+    for copy in outs:
+        copy.wait()
+
+
+def finish_kernel(total_rows, hi_ref, lo_ref, inverse_ref, cross_ref, basis_ref, proj_ref):
     root = float(total_rows) ** 0.5
-
-    @pl.loop(0, chunks)
-    def _(i):
-        part = pl.ds(pl.multiple_of(i * CHUNK, CHUNK), CHUNK)
-        hi = hi_v[part, :]
-        value = dot(hi, inv_hi, 1, 1) + (dot(hi, inv_lo, 1, 1) + dot(lo_v[part, :], inv_hi, 1, 1))
-        basis_ref[part, :] = (value * root).astype(BF16)
-
-    finish(copies)
-    scale = root / total_rows
-
-    @pl.loop(0, blocks)
-    def _(i):
-        block = pl.ds(pl.multiple_of(i * COLS, COLS), COLS)
-        hi, lo = split2(cfull[:, block])
-        proj_ref[:, block] = (dot(inv_hi, hi) + (dot(inv_hi, lo) + dot(inv_lo, hi))) * scale
+    inv_hi, inv_lo = split2(inverse_ref[...])
+    hi = hi_ref[...]
+    value = dot(hi, inv_hi, 1, 1) + (dot(hi, inv_lo, 1, 1) + dot(lo_ref[...], inv_hi, 1, 1))
+    basis_ref[...] = (value * root).astype(BF16)
+    c_hi, c_lo = split2(cross_ref[...])
+    proj_ref[...] = (dot(inv_hi, c_hi) + (dot(inv_hi, c_lo) + dot(inv_lo, c_hi))) * (root / total_rows)
 
 
 def on_device(spectra, omega):
@@ -288,15 +355,24 @@
     n_sa, n_sb = lax.axis_size("sa"), lax.axis_size("sb")
     share = rank // n_sa
     width = features * (share // 8) // n_sb
+    pieces = min(2, width // 128)
+    wide = features // pieces
     vmem = pltpu.VMEM
-    return pl.pallas_call(
-        functools.partial(kernel, n_sa, n_sb),
+    hi, lo, cross, inverse = pl.pallas_call(
+        functools.partial(kernel, n_sa, n_sb, pieces),
         out_shape=(
             jax.ShapeDtypeStruct((rows, rank), BF16),
+            jax.ShapeDtypeStruct((rows, rank), BF16),
             jax.ShapeDtypeStruct((rank, features), F32),
+            jax.ShapeDtypeStruct((rank, rank), F32),
         ),
         in_specs=[pl.BlockSpec(memory_space=pl.ANY), pl.BlockSpec(memory_space=pltpu.VMEM)],
-        out_specs=(pl.BlockSpec(memory_space=pltpu.VMEM), pl.BlockSpec(memory_space=pltpu.VMEM)),
+        out_specs=(
+            pl.BlockSpec(memory_space=pl.ANY),
+            pl.BlockSpec(memory_space=pl.ANY),
+            pl.BlockSpec(memory_space=pl.ANY),
+            pl.BlockSpec(memory_space=pltpu.VMEM),
+        ),
         scratch_shapes=[
             vmem((rows, features), BF16),
             vmem((rows, rank), BF16),
@@ -307,24 +383,46 @@
             vmem((rank, rank), F32),
             vmem((rank, rank), F32),
             vmem((rank, rank), F32),
-            vmem((rank, features), F32),
+            vmem((pieces, rank, wide), F32),
             vmem((n_sa, share, rank), F32),
             vmem((n_sb, share, rank), F32),
             vmem((rank, rank), F32),
-            vmem((n_sa, share, features), F32),
-            vmem((share, features), F32),
-            vmem((n_sb, 8, width), F32),
-            vmem((rank, features), F32),
+            vmem((pieces, rank // 2, wide), F32),
+            vmem((pieces, n_sa // 2, share, wide), F32),
+            vmem((pieces, share, wide), F32),
+            vmem((pieces, n_sb, 8, width // pieces), F32),
+            vmem((pieces, rank, wide), F32),
             vmem((rank, 2 * rank), F32),
-            vmem((rank, rank), F32),
             pltpu.SemaphoreType.DMA((rows // CHUNK,)),
-            pltpu.SemaphoreType.DMA((7, max(n_sa, n_sb))),
-            pltpu.SemaphoreType.DMA((7, max(n_sa, n_sb))),
+            pltpu.SemaphoreType.DMA((2 + pieces,)),
+            pltpu.SemaphoreType.DMA((3 + 6 * pieces, max(n_sa, n_sb))),
+            pltpu.SemaphoreType.DMA((3 + 6 * pieces, max(n_sa, n_sb))),
         ],
         compiler_params=pltpu.CompilerParams(
             collective_id=0, has_side_effects=True, vmem_limit_bytes=52 * 2**20
         ),
     )(spectra, omega)
+    steps = 4
+    tall, slim = rows // steps, features // steps
+    return pl.pallas_call(
+        functools.partial(finish_kernel, rows * n_sa * n_sb),
+        grid=(steps,),
+        out_shape=(
+            jax.ShapeDtypeStruct((rows, rank), BF16),
+            jax.ShapeDtypeStruct((rank, features), F32),
+        ),
+        in_specs=[
+            pl.BlockSpec((tall, rank), lambda i: (i, 0)),
+            pl.BlockSpec((tall, rank), lambda i: (i, 0)),
+            pl.BlockSpec((rank, rank), lambda i: (0, 0)),
+            pl.BlockSpec((rank, slim), lambda i: (0, i)),
+        ],
+        out_specs=(
+            pl.BlockSpec((tall, rank), lambda i: (i, 0)),
+            pl.BlockSpec((rank, slim), lambda i: (0, i)),
+        ),
+        compiler_params=pltpu.CompilerParams(vmem_limit_bytes=40 * 2**20),
+    )(hi, lo, inverse, cross)
 
 
 def solution(mesh):

time: 66.5 us -> 53.8 us (0.81)
  Pallas kernels: 61.6 us -> 49.7 us
  local copies, waits for them, and re-layouts: 4.01 us -> 3.17 us
    pallas_call x1 -> x2, Pallas kernels: 61.6 us -> 49.7 us  [the longest x1 45.7 us: on_device(): pl.pallas_call(functools.partial(kernel, n_sa, n_sb, pieces), out_shape=(...]
    unnamed x2 -> x4, local copies, waits for them, and re-layouts: 4.01 us -> 3.17 us
where the time goes in v2:
time: 53.8 us; the launch traced here: 53.5 us
  Pallas kernels  49.7 us (92%)
  local copies, waits for them, and re-layouts  3.17 us (6%)
  between operations  0.65 us (1%)
    pallas_call x1, Pallas kernels, on_device(): pl.pallas_call(functools.partial(kernel, n_sa, n_sb, pieces), out_shape=(...  45.7 us
    pallas_call x1, Pallas kernels, on_device(): pl.pallas_call(functools.partial(finish_kernel, rows * n_sa * n_sb), grid...  3.98 us
    unnamed x4, local copies, waits for them, and re-layouts  3.17 us

profile of v2, /device:TPU:1, one launch (start us, length us, event | category | flops | bytes accessed | tf_op | source)
XLA Modules:
  0.0 53.5 jit_solution(13223233240017171951)
XLA Ops:
  0.6 45.7 %shard_map.41 = (bf16[4096,256]{1,0:T(8,128)(2,1)}, bf16[4096,256]{1,0:T(8,128)(2,1)}, f32[256,1024]{1,0:T(8,128)S(1)}, f32[256,256]{1,0:T(8,128)S(1)}) custom-call(bf16[4096,1024]{1,0:T(8,128)(2,1)} %x_hbm.1, s32[1024,256]{1,0:T(8,128)} %omega_ref.1), custom_call_target="tpu_custom_call" | custom-call | tf_op jit(solution)/shard_map/pallas_call | solution.py:361
  46.3 0.0 copy-start
  46.3 1.6 %copy-done = bf16[4096,256]{1,0:T(8,128)(2,1)S(1)} copy-done((bf16[4096,256]{1,0:T(8,128)(2,1)S(1)}, bf16[4096,256]{1,0:T(8,128)(2,1)}, u32[]{:S(2)}) %copy-start) | copy-done | bytes 2097176
  47.9 0.0 copy-start.1
  47.9 1.6 %copy-done.1 = bf16[4096,256]{1,0:T(8,128)(2,1)S(1)} copy-done((bf16[4096,256]{1,0:T(8,128)(2,1)S(1)}, bf16[4096,256]{1,0:T(8,128)(2,1)}, u32[]{:S(2)}) %copy-start.1) | copy-done | bytes 2097176
  49.5 4.0 %shard_map.42 = (bf16[4096,256]{1,0:T(8,128)(2,1)}, f32[256,1024]{1,0:T(8,128)}) custom-call(bf16[4096,256]{1,0:T(8,128)(2,1)S(1)} %copy-done, bf16[4096,256]{1,0:T(8,128)(2,1)S(1)} %copy-done.1, f32[256,256]{1,0:T(8,128)S(1)} %get-tuple-element.8.inverse_ref, f32[256,1024]{1,0:T(8,128)S(1)} %get-tuple-element.9.cross_ref), custom_call_target="tpu_custom_call" | custom-call | tf_op jit(solution)/shard_map/pallas_call | solution.py:407
Async XLA Ops:
  46.3 1.6 %copy-start = (bf16[4096,256]{1,0:T(8,128)(2,1)S(1)}, bf16[4096,256]{1,0:T(8,128)(2,1)}, u32[]{:S(2)}) copy-start(bf16[4096,256]{1,0:T(8,128)(2,1)} %get-tuple-element.6.hi_ref) | copy-start | bytes 6291460
  47.9 1.6 %copy-start.1 = (bf16[4096,256]{1,0:T(8,128)(2,1)S(1)}, bf16[4096,256]{1,0:T(8,128)(2,1)}, u32[]{:S(2)}) copy-start(bf16[4096,256]{1,0:T(8,128)(2,1)} %get-tuple-element.7.lo_ref) | copy-start | bytes 6291460

commit v3 on v2

--- a/solution.py
+++ b/solution.py
@@ -11,7 +11,7 @@
 BF16 = jnp.bfloat16
 PANEL = 32
 LEAF = 8
-CHUNK = 512
+CHUNK = 1024
 COLS = 256
 
 
@@ -129,9 +129,9 @@
 
 def kernel(
     n_sa, n_sb, pieces,
-    x_hbm, omega_ref, hi_out, lo_out, cross_out, inverse,
-    x_v, hi_v, lo_v, hit_v, lot_v, om_v, hh_v, hl_v, gram_v, cross_v,
-    gbuf, zbuf, gfull, pairbuf, cbuf, cpart, czbuf, cfull, work,
+    x_hbm, omega_ref, basis_out, proj_ref,
+    x_v, hi_v, lo_v, both_v, om_v, grams_v, gram_v, cross_v,
+    gbuf, zbuf, gfull, pairbuf, cbuf, cpart, czbuf, cfull, work, inverse, basis_v,
     x_sem, out_sem, send_sem, recv_sem,
 ):
     rows, features = x_hbm.shape
@@ -187,8 +187,7 @@
         )
 
     om_v[...] = omega_ref[...].astype(F32).astype(BF16)
-    hh_v[...] = jnp.zeros_like(hh_v)
-    hl_v[...] = jnp.zeros_like(hl_v)
+    grams_v[...] = jnp.zeros_like(grams_v)
 
     @pl.loop(0, chunks)
     def _(i):
@@ -199,17 +198,9 @@
         hi_t, lo_t = split2(sketch.T)
         hi_v[part, :] = hi
         lo_v[part, :] = lo
-        hit_v[:, part] = hi_t
-        lot_v[:, part] = lo_t
-        hh_v[...] += dot(hi_t, hi)
-        hl_v[...] += dot(hi_t, lo)
-
-    outs = [
-        pltpu.make_async_copy(hi_v, hi_out, out_sem.at[0]),
-        pltpu.make_async_copy(lo_v, lo_out, out_sem.at[1]),
-    ]
-    for copy in outs:
-        copy.start()
+        both_t = jnp.concatenate([hi_t, lo_t], axis=0)
+        both_v[:, part] = both_t
+        grams_v[...] += dot(both_t, hi)
 
     def cut(i):
         return pl.ds(pl.multiple_of(i * share, share), share)
@@ -220,7 +211,8 @@
             value = value + buffer[i]
         return value
 
-    gram_v[...] = hh_v[...] + (hl_v[...] + hl_v[...].T)
+    small = grams_v[rank:, :]
+    gram_v[...] = grams_v[:rank, :] + (small + small.T)
     pl.semaphore_wait(barrier, n_sa - 1 + n_sb - 1)
     gram_copies = start(0, "sa", n_sa, a_me, lambda t: gram_v.at[cut(t)], gbuf.at[a_me])
     gbuf[a_me] = gram_v[cut(a_me), :]
@@ -251,7 +243,8 @@
             for block in range(h * wide, (h + 1) * wide, COLS):
                 x = x_v[:, block : block + COLS]
                 part = slice(block - h * wide, block - h * wide + COLS)
-                cross_v[h, :, part] = dot(hit_v[...], x) + dot(lot_v[...], x)
+                both = dot(both_v[...], x)
+                cross_v[h, :, part] = both[:rank] + both[rank:]
             return start(
                 base, "sa", 2, core, lambda t: product.at[half_of(t)], pairbuf.at[h], lambda t: 2 * chip + t
             )
@@ -302,16 +295,14 @@
         def _(k):
             factor_step(k, work, inverse)
 
-    advance(0, 0)
+    advance(0)
     finish(gram_copies)
     zbuf[b_me] = total(gbuf, n_sa)
     gram_copies = start(1, "sb", n_sb, b_me, lambda t: zbuf.at[b_me], zbuf.at[b_me])
-    advance(1, 0)
-    advance(0, 1)
+    advance(1)
     finish(gram_copies)
     gfull[cut(a_me), :] = total(zbuf, n_sb)
     gram_copies = start(2, "sa", n_sa, a_me, lambda t: gfull.at[cut(a_me)], gfull.at[cut(a_me)])
-    advance(1, 1)
     advance(2, 0)
     finish(gram_copies)
     factor_init(gfull[...], work)
@@ -326,27 +317,29 @@
     factor(5, 6)
     advance(5, 0)
     factor(6, panels)
+    root = float(rows * n_sa * n_sb) ** 0.5
+    inv_hi, inv_lo = split2(inverse[...])
+
+    def basis_copy(i):
+        return pltpu.make_async_copy(basis_v.at[chunk(i)], basis_out.at[chunk(i)], out_sem.at[i])
+
+    @pl.loop(0, chunks)
+    def _(i):
+        hi = hi_v[chunk(i), :]
+        value = dot(hi, inv_hi, 1, 1) + (dot(hi, inv_lo, 1, 1) + dot(lo_v[chunk(i), :], inv_hi, 1, 1))
+        basis_v[chunk(i), :] = (value * root).astype(BF16)
+        basis_copy(i).start()
+
     advance(5, 1)
+    scale = root / (rows * n_sa * n_sb)
     for h in range(pieces):
         finish(flight[h])
-        outs.append(
-            pltpu.make_async_copy(
-                cfull.at[h], cross_out.at[:, pl.ds(h * wide, wide)], out_sem.at[2 + h]
-            )
-        )
-        outs[-1].start()
-    for copy in outs:
-        copy.wait()
-
-
-def finish_kernel(total_rows, hi_ref, lo_ref, inverse_ref, cross_ref, basis_ref, proj_ref):
-    root = float(total_rows) ** 0.5
-    inv_hi, inv_lo = split2(inverse_ref[...])
-    hi = hi_ref[...]
-    value = dot(hi, inv_hi, 1, 1) + (dot(hi, inv_lo, 1, 1) + dot(lo_ref[...], inv_hi, 1, 1))
-    basis_ref[...] = (value * root).astype(BF16)
-    c_hi, c_lo = split2(cross_ref[...])
-    proj_ref[...] = (dot(inv_hi, c_hi) + (dot(inv_hi, c_lo) + dot(inv_lo, c_hi))) * (root / total_rows)
+        c_hi, c_lo = split2(cfull[h])
+        proj_ref[:, h * wide : (h + 1) * wide] = (
+            dot(inv_hi, c_hi) + (dot(inv_hi, c_lo) + dot(inv_lo, c_hi))
+        ) * scale
+    for i in range(chunks):
+        basis_copy(i).wait()
 
 
 def on_device(spectra, omega):
@@ -358,18 +351,14 @@
     pieces = min(2, width // 128)
     wide = features // pieces
     vmem = pltpu.VMEM
-    hi, lo, cross, inverse = pl.pallas_call(
+    return pl.pallas_call(
         functools.partial(kernel, n_sa, n_sb, pieces),
         out_shape=(
             jax.ShapeDtypeStruct((rows, rank), BF16),
-            jax.ShapeDtypeStruct((rows, rank), BF16),
             jax.ShapeDtypeStruct((rank, features), F32),
-            jax.ShapeDtypeStruct((rank, rank), F32),
         ),
         in_specs=[pl.BlockSpec(memory_space=pl.ANY), pl.BlockSpec(memory_space=pltpu.VMEM)],
         out_specs=(
-            pl.BlockSpec(memory_space=pl.ANY),
-            pl.BlockSpec(memory_space=pl.ANY),
             pl.BlockSpec(memory_space=pl.ANY),
             pl.BlockSpec(memory_space=pltpu.VMEM),
         ),
@@ -377,11 +366,9 @@
             vmem((rows, features), BF16),
             vmem((rows, rank), BF16),
             vmem((rows, rank), BF16),
-            vmem((rank, rows), BF16),
-            vmem((rank, rows), BF16),
+            vmem((2 * rank, rows), BF16),
             vmem((features, rank), BF16),
-            vmem((rank, rank), F32),
-            vmem((rank, rank), F32),
+            vmem((2 * rank, rank), F32),
             vmem((rank, rank), F32),
             vmem((pieces, rank, wide), F32),
             vmem((n_sa, share, rank), F32),
@@ -393,8 +380,10 @@
             vmem((pieces, n_sb, 8, width // pieces), F32),
             vmem((pieces, rank, wide), F32),
             vmem((rank, 2 * rank), F32),
+            vmem((rank, rank), F32),
+            vmem((rows, rank), BF16),
             pltpu.SemaphoreType.DMA((rows // CHUNK,)),
-            pltpu.SemaphoreType.DMA((2 + pieces,)),
+            pltpu.SemaphoreType.DMA((rows // CHUNK,)),
             pltpu.SemaphoreType.DMA((3 + 6 * pieces, max(n_sa, n_sb))),
             pltpu.SemaphoreType.DMA((3 + 6 * pieces, max(n_sa, n_sb))),
         ],
@@ -402,27 +391,6 @@
             collective_id=0, has_side_effects=True, vmem_limit_bytes=52 * 2**20
         ),
     )(spectra, omega)
-    steps = 4
-    tall, slim = rows // steps, features // steps
-    return pl.pallas_call(
-        functools.partial(finish_kernel, rows * n_sa * n_sb),
-        grid=(steps,),
-        out_shape=(
-            jax.ShapeDtypeStruct((rows, rank), BF16),
-            jax.ShapeDtypeStruct((rank, features), F32),
-        ),
-        in_specs=[
-            pl.BlockSpec((tall, rank), lambda i: (i, 0)),
-            pl.BlockSpec((tall, rank), lambda i: (i, 0)),
-            pl.BlockSpec((rank, rank), lambda i: (0, 0)),
-            pl.BlockSpec((rank, slim), lambda i: (0, i)),
-        ],
-        out_specs=(
-            pl.BlockSpec((tall, rank), lambda i: (i, 0)),
-            pl.BlockSpec((rank, slim), lambda i: (0, i)),
-        ),
-        compiler_params=pltpu.CompilerParams(vmem_limit_bytes=40 * 2**20),
-    )(hi, lo, inverse, cross)
 
 
 def solution(mesh):

time: 53.8 us -> 52.2 us (0.970)
  Pallas kernels: 49.7 us -> 47.3 us
  local copies, waits for them, and re-layouts: 3.17 us -> 4.01 us
    pallas_call x1 -> x0, Pallas kernels: 3.98 us -> none  [on_device(): pl.pallas_call(functools.partial(finish_kernel, rows * n_sa * n_sb), grid...]
    pallas_call x1, Pallas kernels: 45.7 us -> 47.3 us  [on_device(): pl.pallas_call(functools.partial(kernel, n_sa, n_sb, pieces), out_shape=(...]
    unnamed x4 -> x2, local copies, waits for them, and re-layouts: 3.17 us -> 4.01 us
where the time goes in v3:
time: 52.2 us; the launch traced here: 51.9 us
  Pallas kernels  47.3 us (91%)
  local copies, waits for them, and re-layouts  4.01 us (8%)
  between operations  0.64 us (1%)
    pallas_call x1, Pallas kernels, on_device(): pl.pallas_call(functools.partial(kernel, n_sa, n_sb, pieces), out_shape=(...  47.3 us
    unnamed x2, local copies, waits for them, and re-layouts  4.01 us

profile of v3, /device:TPU:1, one launch (start us, length us, event | category | flops | bytes accessed | tf_op | source)
XLA Modules:
  0.0 51.9 jit_solution(8822863386874116687)
XLA Ops:
  0.6 47.3 %shard_map.41 = (bf16[4096,256]{1,0:T(8,128)(2,1)}, f32[256,1024]{1,0:T(8,128)S(1)}) custom-call(bf16[4096,1024]{1,0:T(8,128)(2,1)} %x_hbm.1, s32[1024,256]{1,0:T(8,128)} %omega_ref.1), custom_call_target="tpu_custom_call" | custom-call | tf_op jit(solution)/shard_map/pallas_call | solution.py:354
  47.9 3.0 %copy.6 = bf16[4096,256]{1,0:T(8,128)(2,1)} copy(bf16[4096,256]{1,0:T(8,128)(2,1)} %get-tuple-element.4) | data formatting | bytes 4194304
  51.0 1.0 %copy.7 = f32[256,1024]{1,0:T(8,128)} copy(f32[256,1024]{1,0:T(8,128)S(1)} %get-tuple-element.5) | data formatting | bytes 2097152
